TPU v7x, 256 devices: a whole 4x4x8 slice. The times are simulated.
256 devices in a mesh: depth: 2 (over x_lo), row: 4 (over y), col: 32 (over z, x_hi, core).
Axes of the slice: x: 4 (x_hi: 2, x_lo: 2; x = x_hi * 2 + x_lo), y: 4, z: 8, core: 2. Of those that a mesh axis runs over, the one named last changes fastest.
Arguments:
- object_field: float32 [2, 2, 2048, 16384], P('depth', None, 'row', 'col'), may hold values from -1 to 1.9
- probe: bfloat16 [2, 256, 256], replicated, may hold values from -4 to 4
- amplitude: bfloat16 [4, 32, 2, 256, 256], P('row', 'col'), may hold values from 0.19921875 to 1.59375
- positions: int32 [4, 32, 2, 2], P('row', 'col'), may hold values from 0 to 512, as said below
- live: int32 [4, 32, 2], P('row', 'col'), may hold values from 0 to 1
Outputs:
- object_grad: float32 [2, 2, 2048, 16384], P('depth', None, 'row', 'col')
Inputs may be any that keep to these rules, and one draw needn't show every extreme that they name: `positions`: offsets of a patch's corner inside its tile's region widened by 128 cells on every side.
All inputs are finite; a program needn't handle non-finite values.
Results may differ from a plain program's by a relative error of at most 0.009.
Values may be sent and summed in bfloat16 or wider, within the bound.
A program may use at most 64 MiB of HBM per device.

v0:
```python
import functools
import math

import jax
import jax.numpy as jnp
import ml_dtypes
import numpy as np
from jax import lax
from jax.experimental import pallas as pl
from jax.experimental.pallas import tpu as pltpu
from jax.sharding import PartitionSpec as P

MESH = pl.DeviceIdType.MESH
SCALE = 16384.0
F32 = jnp.float32
BF16 = jnp.bfloat16


def split(values):
    high = values.astype(ml_dtypes.bfloat16)
    low = (values - high.astype(np.float64)).astype(ml_dtypes.bfloat16)
    return high, low


def tables(size):
    steps = np.arange(size)
    angles = 2.0 * math.pi * ((steps[:, None] * steps[None, :]) % size) / size
    fourier = np.exp(-1j * angles) / math.sqrt(size)
    frequency = (steps + size // 2) % size - size // 2
    chirp = np.exp(-1j * math.pi * frequency.astype(np.float64) ** 2 / (2.0 * size))
    spread = fourier.conj() @ (chirp[:, None] * fourier)
    half = size // 2
    same, swapped = spread[:half, :half], spread[:half, half:]
    left, right = [], []
    for table in (fourier[0::2, :half], fourier[1::2, :half], (same + swapped) / 2, (same - swapped) / 2):
        whole = np.block([[table.real, -table.imag], [table.imag, table.real]])
        high, low = split(whole)
        left.append(np.concatenate((high, low, high), axis=1))
        right.append(np.concatenate((high.T, low.T, high.T), axis=0))
    return np.stack(left), np.stack(right)


def dot(left, right):
    return jnp.dot(left, right, preferred_element_type=F32)


def halves(values):
    high = values.astype(BF16)
    return high, (values - high.astype(F32)).astype(BF16)


def kernel(
    tile, patch, n_row, n_col,
    pos, live, obj_hbm, probe_hbm, amp_hbm, left_hbm, right_hbm, out,
    edge, obj, probe, amp, turned_amp, pad, ring, win, wave, grads, gpad, got_x, got_y, got_c,
    left3, right3, pick_rows, pick_cols, put_rows, put_cols, quad_rows, quad_cols, spread,
    in_sem, halo_send, halo_recv, swap_send, swap_recv, rim_send, rim_recv,
):
    rim = patch // 2
    full = tile + patch
    span = patch + rim
    depth, row, col = lax.axis_index("depth"), lax.axis_index("row"), lax.axis_index("col")
    partner = (1 - depth, row, col)

    odd = lax.rem(col, 2)
    away = 2 * odd - 1
    mate = (depth, row, col - away)
    cross = (depth, row, lax.rem(col + away + n_col, n_col))
    along = [(depth, lax.rem(row + step + n_row, n_row), col) for step in (-1, 1)]

    def send(source, target, sems, index, device):
        copy = pltpu.make_async_remote_copy(
            src_ref=source, dst_ref=target, send_sem=sems[0].at[index],
            recv_sem=sems[1].at[index], device_id=device, device_id_type=MESH,
        )
        copy.start()
        return copy

    barrier = pltpu.get_barrier_semaphore()
    for device in (mate, cross, *along, partner):
        pl.semaphore_signal(barrier, inc=1, device_id=device, device_id_type=MESH)
    last = tile // rim
    near_mate, near_cross = pl.ds(rim * (last - (last - 1) * odd), rim), pl.ds(rim * (1 + (last - 1) * odd), rim)
    past_mate, past_cross = pl.ds(rim * ((last + 1) * (1 - odd)), rim), pl.ds(rim * ((last + 1) * odd), rim)
    middle = pl.ds(rim, tile)
    inner_rows = (pl.ds(rim, rim), pl.ds(tile, rim))
    outer_rows = (pl.ds(rim + tile, rim), pl.ds(0, rim))
    halo_sems = (halo_send, halo_recv)
    edge_cross, edge_mate = pl.ds(rim * (last - 1) * odd, rim), pl.ds(rim * (last - 1) * (1 - odd), rim)
    loads = [
        pltpu.make_async_copy(source, target, in_sem.at[index])
        for index, (source, target) in enumerate((
            (obj_hbm.at[0, 0], obj.at[0]), (obj_hbm.at[0, 1], obj.at[1]),
            (left_hbm, left3), (probe_hbm, probe), (amp_hbm.at[0, 0], amp),
            (obj_hbm.at[0, :, :, edge_cross], edge), (right_hbm, right3),
        ))
    ]
    for load in (loads[5], *loads[:5], loads[6]):
        load.start()

    def fixed_point(values):
        return jnp.round(values * SCALE).astype(jnp.int32).astype(jnp.int16)

    loads[5].wait()
    for part in range(2):
        pad[part, middle, near_cross] = fixed_point(edge[part])
    pl.semaphore_wait(barrier, 5)
    halo = [
        send(pad.at[:, rows, near_cross], pad.at[:, rows, past_mate], halo_sems, index, cross)
        for index, rows in enumerate((*inner_rows, pl.ds(2 * rim, tile - 2 * rim)))
    ]
    for part in range(2):
        loads[part].wait()
        pad[part, middle, 2 * rim:tile] = fixed_point(obj[part, :, rim:tile - rim])
        pad[part, middle, near_mate] = fixed_point(obj[part, :, edge_mate])
    halo += [
        send(pad.at[:, inner_rows[k], middle], ring.at[k, :, :, middle], halo_sems, 3 + k, along[k])
        for k in range(2)
    ]
    halo.append(send(pad.at[:, middle, near_mate], pad.at[:, middle, past_cross], halo_sems, 5, mate))

    def halved(values, axis):
        if axis == 0:
            return values[0:rim], values[rim:]
        return values[:, 0:rim], values[:, rim:]

    def stacked(real, imag, axis, mix):
        (real0, real1), (imag0, imag1) = halved(real, axis), halved(imag, axis)
        if mix:
            real0, real1 = real0 + real1, real0 - real1
            imag0, imag1 = imag0 + imag1, imag0 - imag1
        return [jnp.concatenate(pair, axis=axis) for pair in ((real0, imag0), (real1, imag1))]

    def unstacked(first, second, axis, mix):
        (real0, imag0), (real1, imag1) = halved(first, axis), halved(second, axis)
        if mix:
            real0, real1 = real0 + real1, real0 - real1
            imag0, imag1 = imag0 + imag1, imag0 - imag1
        return [jnp.concatenate(pair, axis=axis) for pair in ((real0, real1), (imag0, imag1))]

    def transform3(real, imag, base, mix_after):
        for axis in range(2):
            sides = []
            for place, values in enumerate(stacked(real, imag, axis, True)):
                high, low = halves(values)
                values = jnp.concatenate((high, high, low), axis=axis)
                if axis == 0:
                    sides.append(dot(left3[base + place], values))
                else:
                    sides.append(dot(values, right3[base + place]))
            real, imag = unstacked(*sides, axis, mix_after)
        return real, imag

    def conjugate1(real, imag, base, mix_before):
        for axis in range(2):
            sides = []
            for place, values in enumerate(stacked(real, imag, axis, mix_before)):
                values = values.astype(BF16)
                if axis == 0:
                    sides.append(dot(right3[base + place, 0:patch], values))
                else:
                    sides.append(dot(values, left3[base + place, :, 0:patch]))
            real, imag = unstacked(*sides, axis, True)
        return real, imag

    def one_hot(shape, axis, shift, turn=None):
        index = lax.broadcasted_iota(jnp.int32, shape, 1 - axis)
        if turn is not None:
            index = index + turn
            index = jnp.where(index >= patch, index - patch, index)
        hit = lax.broadcasted_iota(jnp.int32, shape, axis) == index + shift
        return hit.astype(F32).astype(BF16)

    blocks, quads, turned = [], [], []
    for slot in range(2):
        corner = [pos[0, 0, slot, axis] for axis in range(2)]
        turned.append([start < patch for start in corner])
        turns = [jnp.where(flag, rim, 0) for flag in turned[slot]]
        block = [jnp.minimum(start >> 7, (full - span) // 128) for start in corner]
        blocks.append(block)
        pick_rows[slot] = one_hot((rim, span), 1, corner[0] - block[0] * 128, turns[0] + rim)
        pick_cols[slot] = one_hot((span, patch), 0, corner[1] - block[1] * 128, turns[1])
        put_rows[:, slot * patch:(slot + 1) * patch] = one_hot((full, patch), 0, corner[0])
        put_cols[slot] = one_hot((patch, full), 1, corner[1])
        first = [start - rim + turn for start, turn in zip(corner, turns)]
        quad = [jnp.minimum(start >> 7, (tile - patch) // 128) for start in first]
        quads.append(quad)
        quad_rows[slot] = one_hot((rim, patch), 1, first[0] - quad[0] * 128)
        quad_cols[slot] = one_hot((patch, rim), 0, first[1] - quad[1] * 128)

    def select(codes, rows, cols):
        width = codes.shape[1]
        high, low = halves(codes)
        picked = dot(rows, jnp.concatenate((high, low), axis=1)).astype(BF16)
        cells = dot(picked[:, :width], cols) + dot(picked[:, width:], cols)
        return cells.astype(jnp.int32).astype(jnp.int16)

    for slot in range(2):
        for part in range(2):
            block = obj[part, pl.ds(quads[slot][0] * 128, patch), pl.ds(quads[slot][1] * 128, patch)]
            win[depth, slot, part, 0:rim, 0:rim] = select(
                jnp.round(block * SCALE), quad_rows[slot], quad_cols[slot]
            )

    def extract_front(slot, part):
        block = pad[
            part, pl.ds((quads[slot][0] + 1) * 128, patch), pl.ds(blocks[slot][1] * 128, span)
        ]
        cells = select(block.astype(F32), quad_rows[slot], pick_cols[slot, :, rim:])
        win[depth, slot, part, 0:rim, rim:] = cells

    def extract_back(slot, part):
        block = pad[
            part, pl.ds(blocks[slot][0] * 128, span), pl.ds(blocks[slot][1] * 128, span)
        ]
        win[depth, slot, part, rim:] = select(block.astype(F32), pick_rows[slot], pick_cols[slot])

    def swap(buffer, index):
        return pltpu.make_async_remote_copy(
            src_ref=buffer, dst_ref=buffer,
            send_sem=swap_send.at[index], recv_sem=swap_recv.at[index],
            device_id=partner, device_id_type=MESH,
        )

    def patch_of(section, slot):
        parts = []
        for part in range(2):
            codes = win[section, slot, part].astype(F32) * (1.0 / SCALE)
            for axis in range(2):
                front, back = (codes[0:rim], codes[rim:]) if axis == 0 else (codes[:, 0:rim], codes[:, rim:])
                flag = turned[slot][axis]
                codes = jnp.concatenate(
                    (jnp.where(flag, back, front), jnp.where(flag, front, back)), axis=axis
                )
            parts.append(codes)
        return parts

    def swap_piece(slot, section, piece):
        source = win.at[section, slot]
        if piece < 2:
            source = source.at[:, 0:rim, piece * rim:(piece + 1) * rim]
        else:
            source = source.at[pl.ds(piece - 2, 1), rim:patch]
        return swap(source, 4 * slot + piece)

    loads[2].wait()
    loads[3].wait()
    loads[4].wait()
    loads[6].wait()
    place = lax.broadcasted_iota(jnp.int32, (patch, patch), 0)
    order = (
        lax.broadcasted_iota(jnp.int32, (patch, patch), 1)
        == 2 * place - jnp.where(place >= rim, patch - 1, 0)
    ).astype(F32).astype(BF16)
    for slot in range(2):
        rows = dot(order, amp[slot]).astype(BF16)
        turned_amp[slot] = lax.dot_general(
            rows, order, (((1,), (1,)), ((), ())), preferred_element_type=F32
        ).astype(BF16)
    probe_real, probe_imag = probe[0].astype(F32), probe[1].astype(F32)
    for k in range(2):
        halo[k].wait_recv()
        halo.append(
            send(
                pad.at[:, inner_rows[k], past_cross], ring.at[k, :, :, past_cross],
                halo_sems, 6 + k, along[k],
            )
        )
    for slot in range(2):
        swap_piece(slot, depth, 0).start()
    for k in range(2):
        halo[3 + k].wait_recv()
        halo.append(
            send(
                ring.at[k, :, :, near_mate], ring.at[k, :, :, past_cross],
                halo_sems, 8 + k, mate,
            )
        )
    halo[5].wait_recv()
    halo[2].wait_recv()
    for slot in range(2):
        for part in range(2):
            extract_front(slot, part)
        swap_piece(slot, depth, 1).start()
    for copy in halo[6:]:
        copy.wait_recv()
    for k in range(2):
        for part in range(2):
            pad[part, outer_rows[k]] = ring[k, part]

    def propagate(slot):
        obj_real, obj_imag = patch_of(0, slot)
        wave_real, wave_imag = transform3(
            probe_real * obj_real - probe_imag * obj_imag,
            probe_real * obj_imag + probe_imag * obj_real,
            2, True,
        )
        wave[slot, 0] = wave_real.astype(BF16)
        wave[slot, 1] = wave_imag.astype(BF16)

    for slot in range(2):
        for part in range(2):
            extract_back(slot, part)
            swap_piece(slot, depth, 2 + part).start()

    @pl.when(depth == 0)
    def _():
        for slot in range(2):
            propagate(slot)

    for slot in range(2):
        for piece in range(4):
            swap_piece(slot, 1 - depth, piece).wait_recv()

        @pl.when(depth == 1)
        def _():
            propagate(slot)

        wave_real, wave_imag = wave[slot, 0].astype(F32), wave[slot, 1].astype(F32)
        obj_real, obj_imag = patch_of(1, slot)
        far_real, far_imag = transform3(
            wave_real * obj_real - wave_imag * obj_imag,
            wave_real * obj_imag + wave_imag * obj_real,
            0, False,
        )
        power = far_real * far_real + far_imag * far_imag
        weight = live[0, 0, slot].astype(F32)
        factor = weight * (
            1.0 - turned_amp[slot].astype(F32) * lax.rsqrt(jnp.maximum(power, 0.0625))
        )
        back_real, back_imag = conjugate1(far_real * factor, far_imag * factor, 0, False)
        back_real = back_real.astype(BF16).astype(F32)
        back_imag = back_imag.astype(BF16).astype(F32)

        @pl.when(depth == 1)
        def _():
            grads[slot, 0] = (wave_real * back_real + wave_imag * back_imag).astype(BF16)
            grads[slot, 1] = (wave_real * back_imag - wave_imag * back_real).astype(BF16)

        @pl.when(depth == 0)
        def _():
            first_real, first_imag = conjugate1(
                obj_real * back_real + obj_imag * back_imag,
                obj_real * back_imag - obj_imag * back_real,
                2, True,
            )
            first_real = first_real.astype(BF16).astype(F32)
            first_imag = first_imag.astype(BF16).astype(F32)
            grads[slot, 0] = (probe_real * first_real + probe_imag * first_imag).astype(BF16)
            grads[slot, 1] = (probe_real * first_imag - probe_imag * first_real).astype(BF16)

        if slot == 0:
            cells = dot(grads[0].reshape(2 * patch, patch), put_cols[0]).astype(BF16)
            for part in range(2):
                spread[part, 0:patch] = cells[part * patch:(part + 1) * patch]

    outer_cols = jnp.concatenate((put_cols[1, :, 0:rim], put_cols[1, :, rim + tile:]), axis=1)
    outer_ends = jnp.concatenate((put_rows[0:rim], put_rows[rim + tile:]), axis=0)
    last_grads = grads[1].reshape(2 * patch, patch)
    cells = dot(last_grads, outer_cols).astype(BF16)
    for part in range(2):
        spread[part, patch:, 0:rim] = cells[part * patch:(part + 1) * patch, 0:rim]
        spread[part, patch:, rim + tile:] = cells[part * patch:(part + 1) * patch, rim:]
    sides = [(part, place) for place in (past_cross, past_mate) for part in range(2)]
    lanes = jnp.concatenate([spread[part, :, place] for part, place in sides], axis=1)
    cells = dot(outer_ends, lanes).astype(BF16)
    for index, (part, place) in enumerate(sides):
        gpad[part, 0:rim, place] = cells[0:rim, index * rim:(index + 1) * rim]
        gpad[part, rim + tile:, place] = cells[rim:, index * rim:(index + 1) * rim]
    rim_sems = (rim_send, rim_recv)
    edge_rows = (pl.ds(0, rim), pl.ds(rim + tile, rim))
    rims = [
        send(gpad.at[:, edge_rows[k], past_cross], got_c.at[0, k], rim_sems, k, along[k])
        for k in range(2)
    ]
    rims += [
        send(gpad.at[:, edge_rows[k], past_mate], got_c.at[1, k], rim_sems, 2 + k, mate)
        for k in range(2)
    ]
    cells = dot(put_rows[rim:rim + tile], lanes).astype(BF16)
    for index, (part, place) in enumerate(sides):
        gpad[part, middle, place] = cells[:, index * rim:(index + 1) * rim]
    rims.append(
        send(
            gpad.at[:, pl.ds(2 * rim, tile - 2 * rim), past_cross],
            got_x.at[odd, :, pl.ds(rim, tile - 2 * rim)], rim_sems, 4, cross,
        )
    )
    rims.append(send(gpad.at[:, middle, past_mate], got_x.at[1 - odd], rim_sems, 5, mate))

    cells = dot(last_grads, put_cols[1, :, rim:rim + tile]).astype(BF16)
    for part in range(2):
        spread[part, patch:, rim:rim + tile] = cells[part * patch:(part + 1) * patch]
    lanes = jnp.concatenate([spread[part, :, rim:rim + tile] for part in range(2)], axis=1)
    cells = dot(outer_ends, lanes).astype(BF16)
    for part in range(2):
        gpad[part, 0:rim, rim:rim + tile] = cells[0:rim, part * tile:(part + 1) * tile]
        gpad[part, rim + tile:, rim:rim + tile] = cells[rim:, part * tile:(part + 1) * tile]
    rims += [
        send(
            gpad.at[:, edge_rows[k], pl.ds(rim * (1 + odd), tile - rim)],
            got_y.at[k, :, :, pl.ds(rim * odd, tile - rim)], rim_sems, 6 + k, along[k],
        )
        for k in range(2)
    ]
    for k in range(2):
        rims[2 + k].wait_recv()
        for part in range(2):
            total = gpad[part, edge_rows[k], near_mate].astype(F32) + got_c[1, k, part].astype(F32)
            gpad[part, edge_rows[k], near_mate] = total.astype(BF16)
        rims.append(
            send(
                gpad.at[:, edge_rows[k], near_mate], got_y.at[k, :, :, edge_mate],
                rim_sems, 8 + k, along[k],
            )
        )

    for part in range(2):
        out[0, part] = dot(put_rows[rim:rim + tile], spread[part, :, rim:rim + tile])

    tile_rows = (pl.ds(tile - rim, rim), pl.ds(0, rim))
    for k in range(2):
        rims[k].wait_recv()
        rows = inner_rows[1 - k]
        for part in range(2):
            total = gpad[part, rows, past_cross].astype(F32) + got_c[0, k, part].astype(F32)
            gpad[part, rows, past_cross] = total.astype(BF16)
        rims.append(
            send(
                gpad.at[:, rows, past_cross], got_x.at[odd, :, tile_rows[k]],
                rim_sems, 10 + k, cross,
            )
        )
    for copy in rims[4:10]:
        copy.wait_recv()
    core = pl.ds(rim, tile - 2 * rim)
    for part in range(2):
        out[0, part, :, edge_mate] += got_x[odd, part].astype(F32)
        out[0, part, core, edge_cross] += got_x[1 - odd, part, core].astype(F32)
        for k in range(2):
            out[0, part, tile_rows[k]] += got_y[k, part].astype(F32)
    for k in range(2):
        rims[10 + k].wait_recv()
        for part in range(2):
            out[0, part, tile_rows[k], edge_cross] += got_x[1 - odd, part, tile_rows[k]].astype(F32)

    for copy in halo:
        copy.wait_send()
    for slot in range(2):
        for piece in range(4):
            swap_piece(slot, depth, piece).wait_send()
    for copy in rims:
        copy.wait_send()


def on_device(object_field, probe, amplitude, positions, live):
    tile = object_field.shape[2]
    patch = probe.shape[1]
    rim = patch // 2
    full = tile + patch
    left, right = tables(patch)
    vmem = pl.BlockSpec(memory_space=pltpu.VMEM)
    smem = pl.BlockSpec(memory_space=pltpu.SMEM)
    hbm = pl.BlockSpec(memory_space=pl.ANY)
    dma = pltpu.SemaphoreType.DMA
    gradient = pl.pallas_call(
        functools.partial(
            kernel, tile, patch, lax.axis_size("row"), lax.axis_size("col")
        ),
        out_shape=pltpu.VMEM(object_field.shape, F32),
        in_specs=[smem, smem, hbm, hbm, hbm, hbm, hbm],
        out_specs=vmem,
        scratch_shapes=[
            pltpu.VMEM((2, tile, rim), F32),
            pltpu.VMEM((2, tile, tile), F32),
            pltpu.VMEM((2, patch, patch), BF16),
            pltpu.VMEM((2, patch, patch), BF16),
            pltpu.VMEM((2, patch, patch), BF16),
            pltpu.VMEM((2, full, full), jnp.int16),
            pltpu.VMEM((2, 2, rim, full), jnp.int16),
            pltpu.VMEM((2, 2, 2, patch, patch), jnp.int16),
            pltpu.VMEM((2, 2, patch, patch), BF16),
            pltpu.VMEM((2, 2, patch, patch), BF16),
            pltpu.VMEM((2, full, full), BF16),
            pltpu.VMEM((2, 2, tile, rim), BF16),
            pltpu.VMEM((2, 2, rim, tile), BF16),
            pltpu.VMEM((2, 2, 2, rim, rim), BF16),
            pltpu.VMEM(left.shape, BF16),
            pltpu.VMEM(right.shape, BF16),
            pltpu.VMEM((2, rim, patch + rim), BF16),
            pltpu.VMEM((2, patch + rim, patch), BF16),
            pltpu.VMEM((full, 2 * patch), BF16),
            pltpu.VMEM((2, patch, full), BF16),
            pltpu.VMEM((2, rim, patch), BF16),
            pltpu.VMEM((2, patch, rim), BF16),
            pltpu.VMEM((2, 2 * patch, full), BF16),
            dma((7,)), dma((10,)), dma((10,)), dma((8,)), dma((8,)), dma((12,)), dma((12,)),
        ],
        compiler_params=pltpu.CompilerParams(
            collective_id=0, has_side_effects=True, vmem_limit_bytes=56 * 1024 * 1024
        ),
    )(positions, live, object_field, probe, amplitude, jnp.asarray(left), jnp.asarray(right))
    return gradient


def solution(mesh):
    in_specs = (
        P("depth", None, "row", "col"),
        P(),
        P("row", "col", None, None, None),
        P("row", "col", None, None),
        P("row", "col", None),
    )
    out_specs = P("depth", None, "row", "col")
    return jax.shard_map(
        on_device, mesh=mesh, in_specs=in_specs, out_specs=out_specs, check_vma=False
    )
```

profile of v0, /device:TPU:1, one launch (start us, length us, event | category | flops | bytes accessed | tf_op | source)
XLA Modules:
  0.0 39.6 jit_solution(10110742019746646764)
XLA Ops:
  0.0 38.3 %shard_map.73 = f32[1,2,512,512]{3,2,1,0:T(8,128)S(1)} custom-call(s32[1,1,2,2]{3,2,1,0:T(2,128)} %pos.1, s32[1,1,2]{2,1,0:T(1,128)} %live.1, f32[1,2,512,512]{3,2,1,0:T(8,128)} %obj_hbm.1, bf16[2,256,256]{2,1,0:T(8,128)(2,1)} %probe_hbm.1, bf16[1,1,2,256,256]{4,3,2,1,0:T(8,128)(2,1)} %amp_hbm.1, bf16[4,256,768]{2,1,0:T(8,128)(2,1)} %constant.4.clone.left_hbm, ...), custom_call_target="tpu_custom_call" | custom-call | tf_op jit(solution)/shard_map/pallas_call | solution.py:466
  38.3 1.3 %copy.9 = f32[1,2,512,512]{3,2,1,0:T(8,128)} copy(f32[1,2,512,512]{3,2,1,0:T(8,128)S(1)} %shard_map.73) | data formatting | bytes 4194304
where the time goes:
time: 39.7 us; the launch traced here: 39.6 us
  Pallas kernels  38.3 us (96%)
  local copies, waits for them, and re-layouts  1.32 us (3%)
    pallas_call x1, Pallas kernels, on_device(): pl.pallas_call(functools.partial(kernel, tile, patch, lax.axis_size('row'...  38.3 us
    unnamed x1, local copies, waits for them, and re-layouts  1.32 us

commit v1 on v0

--- a/solution.py
+++ b/solution.py
@@ -95,7 +95,7 @@
             (obj_hbm.at[0, :, :, edge_cross], edge), (right_hbm, right3),
         ))
     ]
-    for load in (loads[5], *loads[:5], loads[6]):
+    for load in (loads[5], loads[0], loads[1]):
         load.start()
 
     def fixed_point(values):
@@ -109,6 +109,8 @@
         send(pad.at[:, rows, near_cross], pad.at[:, rows, past_mate], halo_sems, index, cross)
         for index, rows in enumerate((*inner_rows, pl.ds(2 * rim, tile - 2 * rim)))
     ]
+    for load in (*loads[2:5], loads[6]):
+        load.start()
     for part in range(2):
         loads[part].wait()
         pad[part, middle, 2 * rim:tile] = fixed_point(obj[part, :, rim:tile - rim])

time: 39.7 us -> 39.7 us (level)
  no operation moved by 1% of the time
where the time goes in v1:
time: 39.7 us; the launch traced here: 39.6 us
  Pallas kernels  38.3 us (96%)
  local copies, waits for them, and re-layouts  1.32 us (3%)
    pallas_call x1, Pallas kernels, on_device(): pl.pallas_call(functools.partial(kernel, tile, patch, lax.axis_size('row'...  38.3 us
    unnamed x1, local copies, waits for them, and re-layouts  1.32 us

profile of v1, /device:TPU:1, one launch (start us, length us, event | category | flops | bytes accessed | tf_op | source)
XLA Modules:
  0.0 39.6 jit_solution(6674897900102539393)
XLA Ops:
  0.0 38.3 %shard_map.73 = f32[1,2,512,512]{3,2,1,0:T(8,128)S(1)} custom-call(s32[1,1,2,2]{3,2,1,0:T(2,128)} %pos.1, s32[1,1,2]{2,1,0:T(1,128)} %live.1, f32[1,2,512,512]{3,2,1,0:T(8,128)} %obj_hbm.1, bf16[2,256,256]{2,1,0:T(8,128)(2,1)} %probe_hbm.1, bf16[1,1,2,256,256]{4,3,2,1,0:T(8,128)(2,1)} %amp_hbm.1, bf16[4,256,768]{2,1,0:T(8,128)(2,1)} %constant.4.clone.left_hbm, ...), custom_call_target="tpu_custom_call" | custom-call | tf_op jit(solution)/shard_map/pallas_call | solution.py:468
  38.3 1.3 %copy.9 = f32[1,2,512,512]{3,2,1,0:T(8,128)} copy(f32[1,2,512,512]{3,2,1,0:T(8,128)S(1)} %shard_map.73) | data formatting | bytes 4194304

commit v2 on v1

--- a/solution.py
+++ b/solution.py
@@ -417,9 +417,6 @@
             )
         )
 
-    for part in range(2):
-        out[0, part] = dot(put_rows[rim:rim + tile], spread[part, :, rim:rim + tile])
-
     tile_rows = (pl.ds(tile - rim, rim), pl.ds(0, rim))
     for k in range(2):
         rims[k].wait_recv()
@@ -433,6 +430,9 @@
                 rim_sems, 10 + k, cross,
             )
         )
+    for part in range(2):
+        out[0, part] = dot(put_rows[rim:rim + tile], spread[part, :, rim:rim + tile])
+
     for copy in rims[4:10]:
         copy.wait_recv()
     core = pl.ds(rim, tile - 2 * rim)

time: 39.7 us -> 40.8 us (1.028)
  Pallas kernels: 38.3 us -> 39.4 us
    pallas_call x1, Pallas kernels: 38.3 us -> 39.4 us  [on_device(): pl.pallas_call(functools.partial(kernel, tile, patch, lax.axis_size('row'...]
where the time goes in v2:
time: 40.8 us; the launch traced here: 40.7 us
  Pallas kernels  39.4 us (97%)
  local copies, waits for them, and re-layouts  1.32 us (3%)
    pallas_call x1, Pallas kernels, on_device(): pl.pallas_call(functools.partial(kernel, tile, patch, lax.axis_size('row'...  39.4 us
    unnamed x1, local copies, waits for them, and re-layouts  1.32 us

profile of v2, /device:TPU:1, one launch (start us, length us, event | category | flops | bytes accessed | tf_op | source)
XLA Modules:
  0.0 40.7 jit_solution(16216517435971193641)
XLA Ops:
  0.0 39.4 %shard_map.73 = f32[1,2,512,512]{3,2,1,0:T(8,128)S(1)} custom-call(s32[1,1,2,2]{3,2,1,0:T(2,128)} %pos.1, s32[1,1,2]{2,1,0:T(1,128)} %live.1, f32[1,2,512,512]{3,2,1,0:T(8,128)} %obj_hbm.1, bf16[2,256,256]{2,1,0:T(8,128)(2,1)} %probe_hbm.1, bf16[1,1,2,256,256]{4,3,2,1,0:T(8,128)(2,1)} %amp_hbm.1, bf16[4,256,768]{2,1,0:T(8,128)(2,1)} %constant.4.clone.left_hbm, ...), custom_call_target="tpu_custom_call" | custom-call | tf_op jit(solution)/shard_map/pallas_call | solution.py:468
  39.4 1.3 %copy.9 = f32[1,2,512,512]{3,2,1,0:T(8,128)} copy(f32[1,2,512,512]{3,2,1,0:T(8,128)S(1)} %shard_map.73) | data formatting | bytes 4194304

commit v3 on v1

--- a/solution.py
+++ b/solution.py
@@ -191,31 +191,47 @@
         quad_cols[slot] = one_hot((patch, rim), 0, first[1] - quad[1] * 128)
 
     def select(codes, rows, cols):
-        width = codes.shape[1]
-        high, low = halves(codes)
-        picked = dot(rows, jnp.concatenate((high, low), axis=1)).astype(BF16)
-        cells = dot(picked[:, :width], cols) + dot(picked[:, width:], cols)
-        return cells.astype(jnp.int32).astype(jnp.int16)
-
-    for slot in range(2):
-        for part in range(2):
-            block = obj[part, pl.ds(quads[slot][0] * 128, patch), pl.ds(quads[slot][1] * 128, patch)]
-            win[depth, slot, part, 0:rim, 0:rim] = select(
-                jnp.round(block * SCALE), quad_rows[slot], quad_cols[slot]
+        width, height = codes[0].shape[1], rows.shape[0]
+        pieces = [piece for values in codes for piece in halves(values)]
+        picked = dot(rows, jnp.concatenate(pieces, axis=1)).astype(BF16)
+        picked = jnp.concatenate([picked[:, k * width:(k + 1) * width] for k in range(4)], axis=0)
+        cells = dot(picked, cols)
+        cells = [cells[k * height:(k + 1) * height] for k in range(4)]
+        return [
+            (cells[2 * part] + cells[2 * part + 1]).astype(jnp.int32).astype(jnp.int16)
+            for part in range(2)
+        ]
+
+    for slot in range(2):
+        codes = [
+            jnp.round(
+                obj[part, pl.ds(quads[slot][0] * 128, patch), pl.ds(quads[slot][1] * 128, patch)]
+                * SCALE
             )
-
-    def extract_front(slot, part):
-        block = pad[
-            part, pl.ds((quads[slot][0] + 1) * 128, patch), pl.ds(blocks[slot][1] * 128, span)
+            for part in range(2)
         ]
-        cells = select(block.astype(F32), quad_rows[slot], pick_cols[slot, :, rim:])
-        win[depth, slot, part, 0:rim, rim:] = cells
-
-    def extract_back(slot, part):
-        block = pad[
-            part, pl.ds(blocks[slot][0] * 128, span), pl.ds(blocks[slot][1] * 128, span)
+        for part, cells in enumerate(select(codes, quad_rows[slot], quad_cols[slot])):
+            win[depth, slot, part, 0:rim, 0:rim] = cells
+
+    def extract_front(slot):
+        codes = [
+            pad[
+                part, pl.ds((quads[slot][0] + 1) * 128, patch), pl.ds(blocks[slot][1] * 128, span)
+            ].astype(F32)
+            for part in range(2)
         ]
-        win[depth, slot, part, rim:] = select(block.astype(F32), pick_rows[slot], pick_cols[slot])
+        for part, cells in enumerate(select(codes, quad_rows[slot], pick_cols[slot, :, rim:])):
+            win[depth, slot, part, 0:rim, rim:] = cells
+
+    def extract_back(slot):
+        codes = [
+            pad[
+                part, pl.ds(blocks[slot][0] * 128, span), pl.ds(blocks[slot][1] * 128, span)
+            ].astype(F32)
+            for part in range(2)
+        ]
+        for part, cells in enumerate(select(codes, pick_rows[slot], pick_cols[slot])):
+            win[depth, slot, part, rim:] = cells
 
     def swap(buffer, index):
         return pltpu.make_async_remote_copy(
@@ -281,8 +297,7 @@
     halo[5].wait_recv()
     halo[2].wait_recv()
     for slot in range(2):
-        for part in range(2):
-            extract_front(slot, part)
+        extract_front(slot)
         swap_piece(slot, depth, 1).start()
     for copy in halo[6:]:
         copy.wait_recv()
@@ -301,8 +316,8 @@
         wave[slot, 1] = wave_imag.astype(BF16)
 
     for slot in range(2):
+        extract_back(slot)
         for part in range(2):
-            extract_back(slot, part)
             swap_piece(slot, depth, 2 + part).start()
 
     @pl.when(depth == 0)

time: 39.7 us -> 39.7 us (level)
  no operation moved by 1% of the time
where the time goes in v3:
time: 39.7 us; the launch traced here: 39.6 us
  Pallas kernels  38.3 us (96%)
  local copies, waits for them, and re-layouts  1.32 us (3%)
    pallas_call x1, Pallas kernels, on_device(): pl.pallas_call(functools.partial(kernel, tile, patch, lax.axis_size('row'...  38.3 us
    unnamed x1, local copies, waits for them, and re-layouts  1.32 us

profile of v3, /device:TPU:1, one launch (start us, length us, event | category | flops | bytes accessed | tf_op | source)
XLA Modules:
  0.0 39.6 jit_solution(3971379970102765283)
XLA Ops:
  0.0 38.3 %shard_map.73 = f32[1,2,512,512]{3,2,1,0:T(8,128)S(1)} custom-call(s32[1,1,2,2]{3,2,1,0:T(2,128)} %pos.1, s32[1,1,2]{2,1,0:T(1,128)} %live.1, f32[1,2,512,512]{3,2,1,0:T(8,128)} %obj_hbm.1, bf16[2,256,256]{2,1,0:T(8,128)(2,1)} %probe_hbm.1, bf16[1,1,2,256,256]{4,3,2,1,0:T(8,128)(2,1)} %amp_hbm.1, bf16[4,256,768]{2,1,0:T(8,128)(2,1)} %constant.4.clone.left_hbm, ...), custom_call_target="tpu_custom_call" | custom-call | tf_op jit(solution)/shard_map/pallas_call | solution.py:483
  38.3 1.3 %copy.9 = f32[1,2,512,512]{3,2,1,0:T(8,128)} copy(f32[1,2,512,512]{3,2,1,0:T(8,128)S(1)} %shard_map.73) | data formatting | bytes 4194304

commit v4 on v3

--- a/solution.py
+++ b/solution.py
@@ -394,16 +394,16 @@
         send(gpad.at[:, edge_rows[k], past_mate], got_c.at[1, k], rim_sems, 2 + k, mate)
         for k in range(2)
     ]
-    cells = dot(put_rows[rim:rim + tile], lanes).astype(BF16)
-    for index, (part, place) in enumerate(sides):
-        gpad[part, middle, place] = cells[:, index * rim:(index + 1) * rim]
+    cells = dot(put_rows[rim:rim + tile], lanes[:, 0:2 * rim]).astype(BF16)
+    for part in range(2):
+        gpad[part, middle, past_cross] = cells[:, part * rim:(part + 1) * rim]
     rims.append(
         send(
             gpad.at[:, pl.ds(2 * rim, tile - 2 * rim), past_cross],
             got_x.at[odd, :, pl.ds(rim, tile - 2 * rim)], rim_sems, 4, cross,
         )
     )
-    rims.append(send(gpad.at[:, middle, past_mate], got_x.at[1 - odd], rim_sems, 5, mate))
+    mate_lanes = lanes[:, 2 * rim:]
 
     cells = dot(last_grads, put_cols[1, :, rim:rim + tile]).astype(BF16)
     for part in range(2):
@@ -431,6 +431,10 @@
                 rim_sems, 8 + k, along[k],
             )
         )
+    cells = dot(put_rows[rim:rim + tile], mate_lanes).astype(BF16)
+    for part in range(2):
+        gpad[part, middle, past_mate] = cells[:, part * rim:(part + 1) * rim]
+    rims.insert(5, send(gpad.at[:, middle, past_mate], got_x.at[1 - odd], rim_sems, 5, mate))
 
     for part in range(2):
         out[0, part] = dot(put_rows[rim:rim + tile], spread[part, :, rim:rim + tile])

time: 39.7 us -> 40 us (level); the launches traced: 39.6 us -> 39.3 us
  no operation moved by 1% of the time
where the time goes in v4:
time: 40 us; the launch traced here: 39.3 us
  Pallas kernels  38 us (95%)
  local copies, waits for them, and re-layouts  1.32 us (3%)
    pallas_call x1, Pallas kernels, on_device(): pl.pallas_call(functools.partial(kernel, tile, patch, lax.axis_size('row'...  38 us
    unnamed x1, local copies, waits for them, and re-layouts  1.32 us

profile of v4, /device:TPU:1, one launch (start us, length us, event | category | flops | bytes accessed | tf_op | source)
XLA Modules:
  0.0 39.3 jit_solution(4778076415850673243)
XLA Ops:
  0.0 38.0 %shard_map.73 = f32[1,2,512,512]{3,2,1,0:T(8,128)S(1)} custom-call(s32[1,1,2,2]{3,2,1,0:T(2,128)} %pos.1, s32[1,1,2]{2,1,0:T(1,128)} %live.1, f32[1,2,512,512]{3,2,1,0:T(8,128)} %obj_hbm.1, bf16[2,256,256]{2,1,0:T(8,128)(2,1)} %probe_hbm.1, bf16[1,1,2,256,256]{4,3,2,1,0:T(8,128)(2,1)} %amp_hbm.1, bf16[4,256,768]{2,1,0:T(8,128)(2,1)} %constant.4.clone.left_hbm, ...), custom_call_target="tpu_custom_call" | custom-call | tf_op jit(solution)/shard_map/pallas_call | solution.py:487
  38.0 1.3 %copy.9 = f32[1,2,512,512]{3,2,1,0:T(8,128)} copy(f32[1,2,512,512]{3,2,1,0:T(8,128)S(1)} %shard_map.73) | data formatting | bytes 4194304
